TPU v7x, 256 devices: a whole 4x4x8 slice. The times are simulated.
256 devices in a mesh: ctx: 32 (over x, y, core), head: 8 (over z).
Axes of the slice: x: 4, y: 4, z: 8, core: 2. Of those that a mesh axis runs over, the one named last changes fastest.
Arguments:
- queries: bfloat16 [24576, 8192], P('ctx', 'head'), may hold values from -80 to 80
- key_states: bfloat16 [24576, 8192], P('ctx', 'head'), may hold values from -4 to 4
- value_states: bfloat16 [24576, 8192], P('ctx', 'head'), may hold values from -4 to 4
- selection: int32 [512, 2], P('ctx'), may hold values from -1 to 30, as said below
Outputs:
- attended: bfloat16 [24576, 8192], P(('ctx', 'head'))
Inputs may be any that keep to these rules, and one draw needn't show every extreme that they name: For query block b, the rows b * 16 to (b + 1) * 16 - 1 of selection, read row by row, list each of the blocks 0 to b - 1 exactly once in their first b entries, in an order drawn from the seed; all other entries are -1. So no two tiles of one query block list the same key block, and each query block from 1 on lists block 0.
All inputs are finite; a program needn't handle non-finite values.
Results may differ from a plain program's by a relative error of at most 0.0051.
Values may be sent and summed in bfloat16 or wider, within the bound.
A program may use at most 128 MiB of HBM per device.

v0:
```python
import functools
import math

import jax
import jax.numpy as jnp
from jax import lax
from jax.experimental import pallas as pl
from jax.experimental.pallas import tpu as pltpu
from jax.sharding import PartitionSpec as P

HEAD_DIM = 128
TILE = 48
GROUP = 4
UNIT = 16
ROWS = 128
LAG = 2
AHEAD = 2
FLIGHT = 1
NEG = -1e30
SCALE2 = math.log2(math.e) / math.sqrt(HEAD_DIM)
MESH = pl.DeviceIdType.MESH


def loop(low, high, step):
    def once(i, carry):
        step(i)
        return carry

    lax.fori_loop(low, high, once, 0)


def same(a, b):
    return jnp.maximum(1 - jnp.maximum(a - b, b - a), 0)


def by_index(index, count, leaf, fold=8):
    for a in range(0, count, fold):
        def some(_, a=a):
            for i in range(a, a + fold):
                loop(0, same(index, i), lambda _, i=i: leaf(i))

        loop(0, same(index // fold, a // fold), some)


def softmax_parts(scores, values):
    top = jnp.max(scores, axis=1, keepdims=True)
    weights = jnp.exp2((scores - top) * SCALE2).astype(jnp.bfloat16)
    summed = jnp.dot(weights, values, preferred_element_type=jnp.float32)
    total = summed[:, HEAD_DIM:]
    return summed[:, :HEAD_DIM] / total, top * SCALE2 + jnp.log2(total)


def kernel(
    blocks, depth, sel, q_hbm, k_hbm, v_hbm, out,
    q, k, outgoing, arrived, parts, part_lse, back, back_lse, own, own_lse, final, vext, going, onehot, pick, dead, picked_lse,
    fwd_send, fwd_recv, out_send, out_recv, lse_send, lse_recv, z_send, z_recv, load_sem,
):
    me, z = lax.axis_index("ctx"), lax.axis_index("head")
    rows, width = q.shape
    heads = width // HEAD_DIM
    tiles = rows // TILE
    share = rows // depth

    barrier = pltpu.get_barrier_semaphore()
    loop(1, blocks, lambda i: pl.semaphore_signal(
        barrier, inc=1, device_id=(lax.rem(me + i, blocks), z), device_id_type=MESH))
    loop(1, depth, lambda i: pl.semaphore_signal(
        barrier, inc=1, device_id=(me, lax.rem(z + i, depth)), device_id_type=MESH))

    def columns(h):
        return pl.ds(pl.multiple_of(h * HEAD_DIM, HEAD_DIM), HEAD_DIM)

    load_q = pltpu.make_async_copy(q_hbm, q, load_sem.at[heads + 1])
    load_k = pltpu.make_async_copy(k_hbm, k, load_sem.at[heads])
    load_v = [
        pltpu.make_async_copy(
            v_hbm.at[:, h * HEAD_DIM:(h + 1) * HEAD_DIM], vext.at[h, :, :HEAD_DIM], load_sem.at[h])
        for h in range(heads)
    ]
    for copy in [load_q, load_k] + load_v:
        copy.start()

    def shifted(size):
        return (lax.broadcasted_iota(jnp.int32, (TILE, size), 1)
                - lax.broadcasted_iota(jnp.int32, (TILE, size), 0))

    lanes = lax.broadcasted_iota(jnp.int32, (1, HEAD_DIM), 1)

    def choose(c):
        tile = jnp.int32(0)
        for t in range(tiles):
            tile += jnp.where((sel[t, 0] == c) | (sel[t, 1] == c), t, 0)
        here = pl.ds(pl.multiple_of(c * TILE, 16), TILE)
        going[here] = jnp.where(shifted(rows) == tile * TILE, 1.0, 0.0).astype(jnp.bfloat16)

    def select(t):
        for r in range(2):
            i, c = 2 * t + r, sel[t, r]
            here = pl.ds(pl.multiple_of(i * TILE, 16), TILE)
            onehot[here] = jnp.where(shifted(blocks * TILE) == c * TILE, 1.0, 0.0).astype(jnp.bfloat16)
            pick[pl.ds(i, 1)] = jnp.where(lanes == c, 1.0, 0.0)
            dead[pl.ds(i, 1)] = jnp.where(lanes * 0 + c < 0, NEG, 0.0)

    slots = 2 * GROUP
    quads = (me + slots - 1) // slots

    def gather(h):
        def one_quad(j):
            here = pl.ds(pl.multiple_of(j * slots * TILE, 16), slots * TILE)
            tiles_out = jnp.dot(going[here], q[:, columns(h)], preferred_element_type=jnp.float32)
            outgoing[h, pl.ds(j * slots, slots)] = tiles_out.astype(jnp.bfloat16).reshape(slots, TILE, HEAD_DIM)

        loop(0, quads, one_quad)

    loop(0, quads * slots, choose)
    load_q.wait()
    loop(0, FLIGHT, gather)
    pl.semaphore_wait(barrier, blocks - 1 + depth - 1)

    def forward(h, c, slot):
        return pltpu.make_async_remote_copy(
            src_ref=outgoing.at[h, c], dst_ref=arrived.at[h, slot],
            send_sem=fwd_send.at[h], recv_sem=fwd_recv.at[h],
            device_id=(c, z), device_id_type=MESH)

    def backward(h, b, slot):
        return pltpu.make_async_remote_copy(
            src_ref=parts.at[h, b], dst_ref=back.at[h, slot],
            send_sem=out_send.at[h], recv_sem=out_recv.at[h],
            device_id=(b, z), device_id_type=MESH)

    def backward_lse(h, b, slot):
        return pltpu.make_async_remote_copy(
            src_ref=part_lse.at[h, b], dst_ref=back_lse.at[h, slot],
            send_sem=lse_send.at[h], recv_sem=lse_recv.at[h],
            device_id=(b, z), device_id_type=MESH)

    def across(h, other):
        return pltpu.make_async_remote_copy(
            src_ref=final.at[h, pl.ds(pl.multiple_of(other * share, 16), share)],
            dst_ref=out.at[:, columns(z * heads + h)],
            send_sem=z_send.at[h], recv_sem=z_recv.at[h],
            device_id=(me, other), device_id_type=MESH)

    def take(ref, low, high, send_sem, recv_sem):
        slots = ref.at[low:high]
        return pltpu.make_async_remote_copy(
            src_ref=slots, dst_ref=slots, send_sem=send_sem, recv_sem=recv_sem,
            device_id=(lax.rem(me + 1, blocks), z), device_id_type=MESH)

    def send_tiles(h):
        loop(0, me, lambda i: forward(h, me - 1 - i, me).start())

    loop(0, FLIGHT, send_tiles)

    loop(0, quads * GROUP, select)

    def clear(c):
        for h in range(heads):
            back[h, c] = jnp.zeros((TILE, HEAD_DIM), jnp.bfloat16)
            back_lse[h, c] = jnp.zeros((1, HEAD_DIM), jnp.float32)

    loop(me, blocks, clear)

    for h in range(heads):
        vext[h, :, HEAD_DIM:] = jnp.ones((rows, HEAD_DIM), jnp.bfloat16)
    for copy in [load_k] + load_v:
        copy.wait()

    def attend_own(h):
        for r in range(rows // ROWS):
            low, high = r * ROWS, (r + 1) * ROWS
            scores = lax.dot_general(
                q[low:high, columns(h)], k[:high, columns(h)], (((1,), (1,)), ((), ())),
                preferred_element_type=jnp.float32)
            row_ids = low + lax.broadcasted_iota(jnp.int32, scores.shape, 0)
            col_ids = lax.broadcasted_iota(jnp.int32, scores.shape, 1)
            scores = jnp.where(col_ids <= row_ids, scores, NEG)
            own[h, low:high], own_lse[h, low:high] = softmax_parts(scores, vext[h, :high])

    lane = lax.broadcasted_iota(jnp.int32, (TILE, HEAD_DIM), 1)
    row = lax.broadcasted_iota(jnp.int32, (TILE, HEAD_DIM), 0)
    diagonal = lane == row

    def attend_far(h):
        def arrive(m):
            if m + 1 < blocks:
                take(arrived.at[h], m + 1, blocks, fwd_send.at[h], fwd_recv.at[h]).wait_recv()

        by_index(me, blocks, arrive)

        def one_group(first):
            queries = arrived[h, pl.ds(first, GROUP)].reshape(GROUP * TILE, HEAD_DIM)
            scores = lax.dot_general(
                queries, k[:, columns(h)], (((1,), (1,)), ((), ())),
                preferred_element_type=jnp.float32)
            output, lse = softmax_parts(scores, vext[h])
            parts[h, pl.ds(first, GROUP)] = output.astype(jnp.bfloat16).reshape(GROUP, TILE, HEAD_DIM)
            for j in range(GROUP):
                part_lse[h, first + j] = jnp.sum(
                    jnp.where(diagonal, lse[j * TILE:(j + 1) * TILE], 0.0), axis=0, keepdims=True)

        def one_unit(i):
            first = blocks - UNIT * (i + 1)
            for g in range(UNIT // GROUP):
                one_group(first + g * GROUP)

            def send(b):
                backward(h, b, me).start()
                backward_lse(h, b, me).start()

            loop(jnp.maximum(first, me + 1), first + UNIT, send)

        loop(0, (blocks - 1 - me + UNIT - 1) // UNIT, one_unit)

    def combine(h):
        def arrive(m):
            if m:
                take(back.at[h], 0, m, out_send.at[h], out_recv.at[h]).wait_recv()
                take(back_lse.at[h], 0, m, lse_send.at[h], lse_recv.at[h]).wait_recv()

        by_index(me, blocks, arrive)
        picked_lse[...] = dead[...] + jnp.dot(
            pick[:, :blocks], back_lse[h].reshape(blocks, HEAD_DIM),
            precision=lax.Precision.HIGHEST, preferred_element_type=jnp.float32)

        def with_far(j):
            got = jnp.dot(
                onehot[pl.ds(pl.multiple_of(j * slots * TILE, 16), slots * TILE)],
                back[h].reshape(blocks * TILE, HEAD_DIM), preferred_element_type=jnp.float32)
            for t in range(GROUP):
                here = pl.ds(pl.multiple_of((GROUP * j + t) * TILE, 16), TILE)
                outputs, lses = [own[h, here]], [own_lse[h, here]]
                for r in range(2):
                    i = 2 * t + r
                    outputs.append(got[i * TILE:(i + 1) * TILE])
                    spread = jnp.where(diagonal, picked_lse[pl.ds(slots * j + i, 1)], 0.0)
                    lses.append(jnp.sum(spread, axis=1, keepdims=True))
                top = jnp.maximum(jnp.maximum(lses[0], lses[1]), lses[2])
                weights = [jnp.exp2(lse - top) for lse in lses]
                numerator = weights[0] * outputs[0] + weights[1] * outputs[1] + weights[2] * outputs[2]
                final[h, here] = (numerator / (weights[0] + weights[1] + weights[2])).astype(jnp.bfloat16)

        def alone(j):
            here = pl.ds(pl.multiple_of(j * GROUP * TILE, 16), GROUP * TILE)
            final[h, here] = own[h, here].astype(jnp.bfloat16)

        def one_quad(i):
            j = lax.rem(z // 2 + i + 1, tiles // GROUP)

            @pl.when(j < quads)
            def _():
                with_far(j)

            @pl.when(j >= quads)
            def _():
                alone(j)

            def send(other):
                @pl.when(other != z)
                def _():
                    across(h, other).start()

            shares = GROUP * TILE // share
            loop(shares * j, shares * (j + 1), send)

        loop(0, tiles // GROUP, one_quad)
        out[:, columns(z * heads + h)] = final[h, pl.ds(pl.multiple_of(z * share, 16), share)]

    loop(0, AHEAD, attend_own)

    def one_step(h):
        @pl.when(h + FLIGHT < heads)
        def _():
            gather(h + FLIGHT)
            send_tiles(h + FLIGHT)

        @pl.when(h >= LAG)
        def _():
            combine(h - LAG)

        @pl.when(h < heads)
        def _():
            attend_far(h)

        @pl.when(h + AHEAD < heads)
        def _():
            attend_own(h + AHEAD)

    loop(0, heads + LAG, one_step)

    def drain(h):
        def sent(m):
            if m:
                take(outgoing.at[h], 0, m, fwd_send.at[h], fwd_recv.at[h]).wait_send()
            if m + 1 < blocks:
                take(parts.at[h], m + 1, blocks, out_send.at[h], out_recv.at[h]).wait_send()
                take(part_lse.at[h], m + 1, blocks, lse_send.at[h], lse_recv.at[h]).wait_send()

        by_index(me, blocks, sent)
        others = take(final.at[h], 0, (depth - 1) * share, z_send.at[h], z_recv.at[h])
        others.wait_send()
        others.wait_recv()

    loop(0, heads, drain)


def body(blocks, depth, queries, key_states, value_states, selection):
    rows, width = queries.shape
    heads = width // HEAD_DIM
    bf16, f32 = jnp.bfloat16, jnp.float32
    tile_set = pltpu.VMEM((heads, blocks, TILE, HEAD_DIM), bf16)
    lse_set = pltpu.VMEM((heads, blocks, 1, HEAD_DIM), f32)
    dma = pltpu.SemaphoreType.DMA
    vmem, anywhere = pl.BlockSpec(memory_space=pltpu.VMEM), pl.BlockSpec(memory_space=pl.ANY)
    return pl.pallas_call(
        functools.partial(kernel, blocks, depth),
        out_shape=jax.ShapeDtypeStruct((rows // depth, width * depth), bf16),
        in_specs=[pl.BlockSpec(memory_space=pltpu.SMEM), anywhere, anywhere, anywhere],
        out_specs=vmem,
        scratch_shapes=[
            pltpu.VMEM((rows, width), bf16), pltpu.VMEM((rows, width), bf16),
            tile_set, tile_set, tile_set, lse_set, tile_set, lse_set,
            pltpu.VMEM((heads, rows, HEAD_DIM), f32),
            pltpu.VMEM((heads, rows, HEAD_DIM), f32),
            pltpu.VMEM((heads, rows, HEAD_DIM), bf16),
            pltpu.VMEM((heads, rows, 2 * HEAD_DIM), bf16),
            pltpu.VMEM((blocks * TILE, rows), bf16),
            pltpu.VMEM((blocks * TILE, blocks * TILE), bf16),
            pltpu.VMEM((blocks, HEAD_DIM), f32),
            pltpu.VMEM((blocks, HEAD_DIM), f32),
            pltpu.VMEM((blocks, HEAD_DIM), f32),
            *[dma((heads,)) for _ in range(8)],
            dma((heads + 2,)),
        ],
        compiler_params=pltpu.CompilerParams(
            collective_id=0, has_side_effects=True, vmem_limit_bytes=56 * 2**20),
    )(selection, queries, key_states, value_states)


def solution(mesh):
    placed = (P("ctx", "head"), P("ctx", "head"), P("ctx", "head"), P("ctx", None))
    return jax.shard_map(
        functools.partial(body, mesh.shape["ctx"], mesh.shape["head"]),
        mesh=mesh, in_specs=placed, out_specs=P(("ctx", "head"), None), check_vma=False)
```

profile of v0, /device:TPU:2, one launch (start us, length us, event | category | flops | bytes accessed | tf_op | source)
XLA Modules:
  0.0 82.6 jit_solution(14231353842828414590)
XLA Ops:
  0.0 1.4 %copy.5.sel = s32[16,2]{1,0:T(8,128)} copy(s32[16,2]{0,1:T(2,128)} %param.7) | data formatting | bytes 256 | tf_op args[3]
  1.4 78.6 %shard_map.46 = bf16[96,8192]{1,0:T(8,128)(2,1)} custom-call(s32[16,2]{1,0:T(8,128)} %copy.5.sel, bf16[768,1024]{1,0:T(8,128)(2,1)} %q_hbm.1, bf16[768,1024]{1,0:T(8,128)(2,1)} %k_hbm.1, bf16[768,1024]{1,0:T(8,128)(2,1)} %v_hbm.1), custom_call_target="tpu_custom_call" | custom-call | tf_op jit(solution)/shard_map/pallas_call | solution.py:316
  80.0 2.7 %copy.7 = bf16[96,8192]{1,0:T(8,128)(2,1)} copy(bf16[96,8192]{1,0:T(8,128)(2,1)} %shard_map.46) | data formatting | bytes 3145728
where the time goes:
time: 82.8 us; the launch traced here: 82.6 us
  Pallas kernels  78.6 us (95%)
  local copies, waits for them, and re-layouts  4 us (5%)
    pallas_call x1, Pallas kernels, body(): pl.pallas_call(functools.partial(kernel, blocks, depth), out_shape=jax.Sh...  78.6 us
    unnamed x2, local copies, waits for them, and re-layouts  4 us

commit v1 on v0

--- a/solution.py
+++ b/solution.py
@@ -152,6 +152,8 @@
         loop(0, me, lambda i: forward(h, me - 1 - i, me).start())
 
     loop(0, FLIGHT, send_tiles)
+    gather(FLIGHT)
+    send_tiles(FLIGHT)
 
     loop(0, quads * GROUP, select)
 
@@ -270,7 +272,7 @@
     loop(0, AHEAD, attend_own)
 
     def one_step(h):
-        @pl.when(h + FLIGHT < heads)
+        @pl.when((h > 0) & (h + FLIGHT < heads))
         def _():
             gather(h + FLIGHT)
             send_tiles(h + FLIGHT)

time: 82.8 us -> 83.1 us (level)
  no operation moved by 1% of the time
where the time goes in v1:
time: 83.1 us; the launch traced here: 82.9 us
  Pallas kernels  78.9 us (95%)
  local copies, waits for them, and re-layouts  4 us (5%)
    pallas_call x1, Pallas kernels, body(): pl.pallas_call(functools.partial(kernel, blocks, depth), out_shape=jax.Sh...  78.9 us
    unnamed x2, local copies, waits for them, and re-layouts  4 us

profile of v1, /device:TPU:2, one launch (start us, length us, event | category | flops | bytes accessed | tf_op | source)
XLA Modules:
  0.0 82.9 jit_solution(5017002331083834650)
XLA Ops:
  0.0 1.4 %copy.5.sel = s32[16,2]{1,0:T(8,128)} copy(s32[16,2]{0,1:T(2,128)} %param.7) | data formatting | bytes 256 | tf_op args[3]
  1.4 78.9 %shard_map.46 = bf16[96,8192]{1,0:T(8,128)(2,1)} custom-call(s32[16,2]{1,0:T(8,128)} %copy.5.sel, bf16[768,1024]{1,0:T(8,128)(2,1)} %q_hbm.1, bf16[768,1024]{1,0:T(8,128)(2,1)} %k_hbm.1, bf16[768,1024]{1,0:T(8,128)(2,1)} %v_hbm.1), custom_call_target="tpu_custom_call" | custom-call | tf_op jit(solution)/shard_map/pallas_call | solution.py:318
  80.3 2.7 %copy.7 = bf16[96,8192]{1,0:T(8,128)(2,1)} copy(bf16[96,8192]{1,0:T(8,128)(2,1)} %shard_map.46) | data formatting | bytes 3145728
